TPU v7x, 256 devices: a whole 4x4x8 slice. The times are simulated.
256 devices in a mesh: ia: 4 (over x), ja: 8 (over z_hi, y), ka: 8 (over z_lo, core).
Axes of the slice: x: 4, y: 4, z: 8 (z_hi: 2, z_lo: 4; z = z_hi * 4 + z_lo), core: 2. Of those that a mesh axis runs over, the one named last changes fastest.
Arguments:
- inputs: bfloat16 [4, 2048, 4096], P('ia', 'ja', 'ka'), may hold values from -0.0625 to 0.0625
- attn_out: bfloat16 [4, 2048, 4096], P(None, 'ja', ('ia', 'ka')), may hold values from -0.0625 to 0.0625
- grad_out: bfloat16 [4, 2048, 4096], P('ia', 'ja', 'ka'), may hold values from -6 to 6
- grad_query: bfloat16 [4, 2048, 4096], P(None, 'ja', ('ia', 'ka')), may hold values from -6 to 6
- grad_key: bfloat16 [4, 2048, 4096], P(None, 'ja', ('ia', 'ka')), may hold values from -6 to 6
- grad_value: bfloat16 [4, 2048, 4096], P(None, 'ja', ('ia', 'ka')), may hold values from -6 to 6
- query_weight: bfloat16 [4096, 4096], P('ka', ('ia', 'ja')), may hold values from -0.09375 to 0.09375
- key_weight: bfloat16 [4096, 4096], P('ka', ('ia', 'ja')), may hold values from -0.09375 to 0.09375
- value_weight: bfloat16 [4096, 4096], P('ka', ('ia', 'ja')), may hold values from -0.09375 to 0.09375
Outputs:
- grad_inputs: bfloat16 [4, 2048, 4096], P('ia', 'ja', 'ka')
- query_weight_grad: float32 [4096, 4096], P('ka', ('ia', 'ja'))
- key_weight_grad: float32 [4096, 4096], P('ka', ('ia', 'ja'))
- value_weight_grad: float32 [4096, 4096], P('ka', ('ia', 'ja'))
- output_weight_grad: float32 [4096, 4096], P(('ia', 'ja'), 'ka')
All inputs are finite; a program needn't handle non-finite values.
Results may differ from a plain program's by a relative error of at most 0.015.
Values may be sent and summed in bfloat16 or wider, within the bound.
A program may use at most 128 MiB of HBM per device.

v0:
```python
import jax
import jax.numpy as jnp
from jax import lax
from jax.sharding import PartitionSpec as P


def project(grads, weight_piece):
    return jnp.einsum("btf,df->btd", grads, weight_piece, preferred_element_type=jnp.float32)


def fold_weights(query_weight, key_weight, value_weight, folder, initial):
    return folder(
        initial,
        (
            lax.all_gather(query_weight, "ja", axis=1, tiled=True),
            lax.all_gather(key_weight, "ja", axis=1, tiled=True),
            lax.all_gather(value_weight, "ja", axis=1, tiled=True),
        ),
        jnp.int32(0),
    )


def local(
    inputs,
    attn_out,
    grad_out,
    grad_query,
    grad_key,
    grad_value,
    query_weight,
    key_weight,
    value_weight,
):
    rows_all, grad_rows = (
        lax.all_gather(inputs, "ia", axis=0, tiled=True),
        lax.all_gather(grad_out, "ia", axis=0, tiled=True),
    )
    attn_full, query_full, key_full, value_full = (
        lax.all_gather(attn_out, "ka", axis=2, tiled=True),
        lax.all_gather(grad_query, "ka", axis=2, tiled=True),
        lax.all_gather(grad_key, "ka", axis=2, tiled=True),
        lax.all_gather(grad_value, "ka", axis=2, tiled=True),
    )
    query_term = jnp.einsum("btd,btf->df", rows_all, query_full, preferred_element_type=jnp.float32)
    key_term = jnp.einsum("btd,btf->df", rows_all, key_full, preferred_element_type=jnp.float32)
    value_term = jnp.einsum("btd,btf->df", rows_all, value_full, preferred_element_type=jnp.float32)
    output_term = jnp.einsum(
        "btf,btd->fd", attn_full, grad_rows, preferred_element_type=jnp.float32
    )
    query_weight_grad, key_weight_grad, value_weight_grad, output_weight_grad = (
        lax.psum_scatter(
            query_term.astype(jnp.bfloat16), "ja", scatter_dimension=1, tiled=True
        ).astype(jnp.float32),
        lax.psum_scatter(
            key_term.astype(jnp.bfloat16), "ja", scatter_dimension=1, tiled=True
        ).astype(jnp.float32),
        lax.psum_scatter(
            value_term.astype(jnp.bfloat16), "ja", scatter_dimension=1, tiled=True
        ).astype(jnp.float32),
        lax.psum_scatter(
            output_term.astype(jnp.bfloat16), "ja", scatter_dimension=0, tiled=True
        ).astype(jnp.float32),
    )
    grads_all = (query_full, key_full, value_full)
    blank_sum = jnp.zeros(
        (query_full.shape[0], query_full.shape[1], query_weight.shape[0]), jnp.float32
    )

    def add_all(running, pieces, offset):
        for grads, piece_block in zip(grads_all, pieces):
            running = running + project(grads, piece_block)
        return running

    partial_term = fold_weights(query_weight, key_weight, value_weight, add_all, blank_sum)
    owned_sum = lax.psum_scatter(partial_term, "ia", scatter_dimension=0, tiled=True)
    grad_inputs = owned_sum.astype(jnp.bfloat16)
    return (grad_inputs, query_weight_grad, key_weight_grad, value_weight_grad, output_weight_grad)


def solution(mesh):
    return jax.shard_map(
        local,
        mesh=mesh,
        in_specs=(
            P("ia", "ja", "ka"),
            P(None, "ja", ("ia", "ka")),
            P("ia", "ja", "ka"),
            P(None, "ja", ("ia", "ka")),
            P(None, "ja", ("ia", "ka")),
            P(None, "ja", ("ia", "ka")),
            P("ka", ("ia", "ja")),
            P("ka", ("ia", "ja")),
            P("ka", ("ia", "ja")),
        ),
        out_specs=(
            P("ia", "ja", "ka"),
            P("ka", ("ia", "ja")),
            P("ka", ("ia", "ja")),
            P("ka", ("ia", "ja")),
            P(("ia", "ja"), "ka"),
        ),
        check_vma=False,
    )
```

profile of v0, /device:TPU:1, one launch (start us, length us, event | category | flops | bytes accessed | tf_op | source)
XLA Modules:
  0.0 797.3 jit_solution(14225790646146462214)
XLA Ops:
  10.6 1.8 copy.19
  14.7 24.5 %all-gather.22.cloned.1.call-done = bf16[4,256,512]{2,1,0:T(8,128)(2,1)} async-done(((bf16[1,256,512]{2,1,0:T(8,128)(2,1)}), bf16[4,256,512]{2,1,0:T(8,128)(2,1)}) %all-gather.22.cloned.1.call-update) | async-done | bytes 1048592 | tf_op jit(solution)/shard_map/all_gather | solution.py:35
  39.2 42.5 %all-gather.10.cloned.1.call-done = bf16[4,256,1024]{2,1,0:T(8,128)(2,1)} async-done(((bf16[4,256,128]{2,1,0:T(8,128)(2,1)}), bf16[4,256,1024]{2,1,0:T(8,128)(2,1)}) %all-gather.10.cloned.1.call-update) | async-done | bytes 2097168 | tf_op jit(solution)/shard_map/all_gather | solution.py:40
  81.7 3.2 bitcast_convert_fusion.3
  86.3 34.5 %all-gather.14.cloned.1.call-done = bf16[4,256,1024]{2,1,0:T(8,128)(2,1)} async-done(((bf16[4,256,128]{2,1,0:T(8,128)(2,1)}), bf16[4,256,1024]{2,1,0:T(8,128)(2,1)}) %all-gather.14.cloned.1.call-update) | async-done | bytes 2097168 | tf_op jit(solution)/shard_map/all_gather | solution.py:41
  120.8 2.9 bitcast_convert_fusion.2
  125.1 34.7 %all-gather.18.cloned.1.call-done = bf16[4,256,1024]{2,1,0:T(8,128)(2,1)} async-done(((bf16[4,256,128]{2,1,0:T(8,128)(2,1)}), bf16[4,256,1024]{2,1,0:T(8,128)(2,1)}) %all-gather.18.cloned.1.call-update) | async-done | bytes 2097168 | tf_op jit(solution)/shard_map/all_gather | solution.py:42
  159.8 2.9 bitcast_convert_fusion.1
  164.1 20.9 %all-gather.26.cloned.1.call-done = bf16[4,256,512]{2,1,0:T(8,128)(2,1)} async-done(((bf16[1,256,512]{2,1,0:T(8,128)(2,1)}), bf16[4,256,512]{2,1,0:T(8,128)(2,1)}) %all-gather.26.cloned.1.call-update) | async-done | bytes 1048592 | tf_op jit(solution)/shard_map/all_gather | solution.py:36
  185.0 41.0 %all-gather.24.cloned.1.call-done = bf16[4,256,1024]{1,2,0:T(8,128)(2,1)} async-done(((bf16[4,256,128]{1,2,0:T(8,128)(2,1)}), bf16[4,256,1024]{1,2,0:T(8,128)(2,1)}) %all-gather.24.cloned.1.call-update) | async-done | bytes 2097168 | tf_op jit(solution)/shard_map/all_gather | solution.py:39
  226.0 4.1 bitcast_convert_fusion
  230.2 59.7 %all-gather.16.cloned.1.call-done = bf16[512,1024]{1,0:T(8,128)(2,1)} async-done(((bf16[512,128]{1,0:T(8,128)(2,1)}), bf16[512,1024]{1,0:T(8,128)(2,1)}) %all-gather.16.cloned.1.call-update) | async-done | bytes 1048592 | tf_op jit(solution)/shard_map/all_gather | solution.py:16
  290.0 3.9 fusion.1
  293.8 56.0 %all-gather.12.cloned.1.call-done = bf16[512,1024]{1,0:T(8,128)(2,1)} async-done(((bf16[512,128]{1,0:T(8,128)(2,1)}), bf16[512,1024]{1,0:T(8,128)(2,1)}) %all-gather.12.cloned.1.call-update) | async-done | bytes 1048592 | tf_op jit(solution)/shard_map/all_gather | solution.py:15
  349.8 4.5 fusion.3
  354.4 55.3 %all-gather.20.cloned.1.call-done = bf16[512,1024]{1,0:T(8,128)(2,1)} async-done(((bf16[512,128]{1,0:T(8,128)(2,1)}), bf16[512,1024]{1,0:T(8,128)(2,1)}) %all-gather.20.cloned.1.call-update) | async-done | bytes 1048592 | tf_op jit(solution)/shard_map/all_gather | solution.py:17
  409.7 5.2 add_add_fusion
  415.0 80.7 %reduce-scatter.16.cloned.1.call-done = bf16[128,512]{1,0:T(8,128)(2,1)} async-done(((bf16[1024,512]{1,0:T(8,128)(2,1)}), bf16[128,512]{1,0:T(8,128)(2,1)}) %reduce-scatter.16.cloned.1.call-update) | async-done | bytes 131088
  497.4 85.5 %reduce-scatter.18.cloned.1.call-done = bf16[128,512]{1,0:T(8,128)(2,1)} async-done(((bf16[1024,512]{1,0:T(8,128)(2,1)}), bf16[128,512]{1,0:T(8,128)(2,1)}) %reduce-scatter.18.cloned.1.call-update) | async-done | bytes 131088
  584.7 84.8 %reduce-scatter.20.cloned.1.call-done = bf16[128,512]{1,0:T(8,128)(2,1)} async-done(((bf16[1024,512]{1,0:T(8,128)(2,1)}), bf16[128,512]{1,0:T(8,128)(2,1)}) %reduce-scatter.20.cloned.1.call-update) | async-done | bytes 131088
  671.2 85.4 %reduce-scatter.14.cloned.1.call-done = bf16[128,512]{1,0:T(8,128)(2,1)} async-done(((bf16[1024,512]{1,0:T(8,128)(2,1)}), bf16[128,512]{1,0:T(8,128)(2,1)}) %reduce-scatter.14.cloned.1.call-update) | async-done | bytes 131088 | tf_op jit(solution)/shard_map/reduce_scatter | solution.py:60
  756.7 1.6 convert_element_type.35
  758.3 30.7 %reduce-scatter.12.cloned.1.call-done = f32[1,256,512]{2,1,0:T(8,128)} async-done(((f32[4,256,512]{2,1,0:T(8,128)}), f32[1,256,512]{2,1,0:T(8,128)}) %reduce-scatter.12.cloned.1.call-update) | async-done | bytes 524304 | tf_op jit(solution)/shard_map/reduce_scatter | solution.py:75
  788.9 1.8 convert_element_type.27
  (43 shorter events, 15.1 us)
Async XLA Ops:
  7.2 32.1 %all-gather.22.cloned.1.call-start = ((), (), s32[]{:S(2)}) async-start(), calls=%async_computation.12 | async-start | bytes 1310720 | tf_op jit(solution)/shard_map/all_gather | solution.py:35
  7.9 73.8 %all-gather.10.cloned.1.call-start = ((), (), s32[]{:S(2)}) async-start(), calls=%async_computation.5 | async-start | bytes 2359296 | tf_op jit(solution)/shard_map/all_gather | solution.py:40
  8.6 112.2 %all-gather.14.cloned.1.call-start = ((), (), s32[]{:S(2)}) async-start(), calls=%async_computation.7 | async-start | bytes 2359296 | tf_op jit(solution)/shard_map/all_gather | solution.py:41
  9.4 150.4 %all-gather.18.cloned.1.call-start = ((), (), s32[]{:S(2)}) async-start(), calls=%async_computation.9 | async-start | bytes 2359296 | tf_op jit(solution)/shard_map/all_gather | solution.py:42
  10.0 175.0 %all-gather.26.cloned.1.call-start = ((), (), s32[]{:S(2)}) async-start(), calls=%async_computation.14 | async-start | bytes 1310720 | tf_op jit(solution)/shard_map/all_gather | solution.py:36
  10.5 215.5 %all-gather.24.cloned.1.call-start = ((), (), s32[]{:S(2)}) async-start(), calls=%async_computation.13 | async-start | bytes 2359296 | tf_op jit(solution)/shard_map/all_gather | solution.py:39
  12.4 277.5 %all-gather.16.cloned.1.call-start = ((), (), s32[]{:S(2)}) async-start(), calls=%async_computation.8 | async-start | bytes 1179648 | tf_op jit(solution)/shard_map/all_gather | solution.py:16
  13.2 336.7 %all-gather.12.cloned.1.call-start = ((), (), s32[]{:S(2)}) async-start(), calls=%async_computation.6 | async-start | bytes 1179648 | tf_op jit(solution)/shard_map/all_gather | solution.py:15
  13.9 395.8 %all-gather.20.cloned.1.call-start = ((), (), s32[]{:S(2)}) async-start(), calls=%async_computation.10 | async-start | bytes 1179648 | tf_op jit(solution)/shard_map/all_gather | solution.py:17
  14.6 481.0 %reduce-scatter.16.cloned.1.call-start = ((), (), s32[]{:S(2)}) async-start(), calls=%async_computation.16 | async-start | bytes 1179648
  84.9 35.9 %copy-start = (bf16[4,256,512]{2,1,0:T(8,128)(2,1)S(1)}, bf16[4,256,512]{2,1,0:T(8,128)(2,1)}, u32[]{:S(2)}) copy-start(bf16[4,256,512]{2,1,0:T(8,128)(2,1)} %all-gather.22.cloned.1.call-done) | copy-start | bytes 3145732
  86.3 496.7 %reduce-scatter.18.cloned.1.call-start = ((), (), s32[]{:S(2)}) async-start(), calls=%async_computation.17 | async-start | bytes 1179648
  125.1 544.4 %reduce-scatter.20.cloned.1.call-start = ((), (), s32[]{:S(2)}) async-start(), calls=%async_computation.18 | async-start | bytes 1179648
  164.0 125.9 %copy-start.2 = (bf16[4,256,1024]{2,1,0:T(8,128)(2,1)S(1)}, bf16[4,256,1024]{2,1,0:T(8,128)(2,1)}, u32[]{:S(2)}) copy-start(bf16[4,256,1024]{2,1,0:T(8,128)(2,1)} %all-gather.14.cloned.1.call-done) | copy-start | bytes 6291460
  164.0 592.6 %reduce-scatter.14.cloned.1.call-start = ((), (), s32[]{:S(2)}) async-start(), calls=%async_computation.15 | async-start | bytes 1179648 | tf_op jit(solution)/shard_map/reduce_scatter | solution.py:60
  230.2 558.8 %reduce-scatter.12.cloned.1.call-start = ((), (), s32[]{:S(2)}) async-start(), calls=%async_computation.11 | async-start | bytes 2621440 | tf_op jit(solution)/shard_map/reduce_scatter | solution.py:75
  293.8 115.9 %copy-start.1 = (bf16[4,256,1024]{2,1,0:T(8,128)(2,1)S(1)}, bf16[4,256,1024]{2,1,0:T(8,128)(2,1)}, u32[]{:S(2)}) copy-start(bf16[4,256,1024]{2,1,0:T(8,128)(2,1)} %all-gather.18.cloned.1.call-done) | copy-start | bytes 6291460
Sparse Core Ops, SparseCore 0:
  9.8 29.3 all-gather.21
  40.9 40.7 all-gather.9
  83.4 37.3 all-gather.13
  122.4 37.3 all-gather.17
  161.4 23.4 all-gather.25
  187.2 38.7 all-gather.23
  228.5 61.3 all-gather.15
  292.4 57.3 all-gather.11
  352.3 57.3 all-gather.19
  413.5 82.1 reduce-scatter.15
  500.1 82.7 reduce-scatter.17
  586.8 82.6 reduce-scatter.19
  673.9 82.6 reduce-scatter.13
  759.1 29.8 reduce-scatter.11
where the time goes:
time: 798 us; the launch traced here: 797 us
  waiting for transfers between devices  742 us (93%)
  matrix products  26.6 us (3%)
  between operations  14 us (2%)
  local copies, waits for them, and re-layouts  8.9 us (1%)
    unnamed x17, waiting for transfers between devices  256 us
    reduce_scatter x1, waiting for transfers between devices, local(): lax.psum_scatter(output_term.astype(jnp.bfloat16), 'ja', scatter_dimensio...  85.4 us
    all_gather x1, waiting for transfers between devices, fold_weights(): lax.all_gather(key_weight, 'ja', axis=1, tiled=True)  59.7 us
    all_gather x1, waiting for transfers between devices, fold_weights(): lax.all_gather(query_weight, 'ja', axis=1, tiled=True)  56 us
    all_gather x1, waiting for transfers between devices, fold_weights(): lax.all_gather(value_weight, 'ja', axis=1, tiled=True)  55.3 us
    all_gather x1, waiting for transfers between devices, local(): lax.all_gather(grad_query, 'ka', axis=2, tiled=True)  42.5 us
    all_gather x1, waiting for transfers between devices, local(): lax.all_gather(attn_out, 'ka', axis=2, tiled=True)  41 us
    all_gather x1, waiting for transfers between devices, local(): lax.all_gather(grad_value, 'ka', axis=2, tiled=True)  34.7 us
  transfers between devices with their start and end apart: 14, of which 14 were waited for; matrix products, arithmetic and copies ran while one was open for 5% of the time, Pallas kernels for 0%

commit v1 on v0

v1 whole, which is shorter than its diff:
```python
import functools

import jax
import jax.numpy as jnp
from jax import lax
from jax.experimental import pallas as pl
from jax.experimental.pallas import tpu as pltpu
from jax.sharding import PartitionSpec as P

MESH = pl.DeviceIdType.MESH
BF16 = jnp.bfloat16
F32 = jnp.float32
ATTN = 3


def contract_rows(a, b):
    return lax.dot_general(a, b, (((0,), (0,)), ((), ())), preferred_element_type=F32)


def contract_columns(a, b):
    return lax.dot_general(a, b, (((1,), (1,)), ((), ())), preferred_element_type=F32)


def exchange_kernel(
    in_ref, go_ref, gq_ref, gk_ref, gv_ref, at_ref, wq_ref, wk_ref, wv_ref,
    zr, zro, gz, gown,
    xb, gb, wb, ys, yso, yr, yro, zs, zso, xs, xr, gzs, ownv,
    loc_sem, xz_s, xz_r, xo_s, xo_r, xf_s, xf_r,
    gz_s, gz_r, gc_s, gc_r, gf_s, gf_r,
    wz_s, wz_r, wy_s, wy_r, dy_s, dy_r, dz_s, dz_r,
    gx_s, gx_r, gg_s, gg_r,
):
    ia, ja, ka = lax.axis_index("ia"), lax.axis_index("ja"), lax.axis_index("ka")
    x, y, zh = ia, ja % 4, ja // 4
    zl, c = ka // 2, ka % 2
    zl1, zl0 = zl // 2, zl % 2

    def device(x_=None, y_=None, zh_=None, zl_=None, c_=None):
        x_ = x if x_ is None else x_
        y_ = y if y_ is None else y_
        zh_ = zh if zh_ is None else zh_
        zl_ = zl if zl_ is None else zl_
        c_ = c if c_ is None else c_
        return (x_, zh_ * 4 + y_, zl_ * 2 + c_)

    def flip(bit):
        return 1 - bit

    zl_side = zl1 * 2 + flip(zl0)
    zl_far = flip(zl1) * 2 + zl0
    side, far, core = device(zl_=zl_side), device(zl_=zl_far), device(c_=flip(c))
    over, over_far = device(zh_=flip(zh)), device(zh_=flip(zh), zl_=zl_far)
    x_peer = [device(x_=(x + d) % 4) for d in (1, 2, 3)]
    y_peer = [device(y_=(y + d) % 4) for d in (1, 2, 3)]
    near_first = (0, 2, 1)

    def remote(src, dst, send, recv, to):
        return pltpu.make_async_remote_copy(
            src_ref=src, dst_ref=dst, send_sem=send, recv_sem=recv,
            device_id=to, device_id_type=MESH,
        )

    sent = []

    def start(copy):
        copy.start()
        sent.append(copy)

    def lanes(k):
        return pl.ds(pl.multiple_of(k * 128, 128), 128)

    def bank(b):
        return pl.ds(pl.multiple_of(b * 256, 256), 256)

    g_refs = (gq_ref, gk_ref, gv_ref, at_ref)
    w_refs = (wq_ref, wk_ref, wv_ref)
    x_refs = (in_ref, go_ref)
    k_own, k_side = zl0 * 2 + c, flip(zl0) * 2 + c

    def own_g(a):
        return pltpu.make_async_copy(g_refs[a], gb.at[a, :, lanes(k_own)], loc_sem.at[a])

    def own_x(t):
        return pltpu.make_async_copy(x_refs[t], xb.at[t, zl1, bank(x)], loc_sem.at[4 + t])

    for a in (ATTN, 0, 1, 2):
        own_g(a).start()
    for t in (1, 0):
        own_x(t).start()

    def g_side(a):
        return remote(g_refs[a], gb.at[a, :, lanes(k_own)], gz_s.at[a], gz_r.at[a], side)

    def g_core(a):
        return remote(g_refs[a], gb.at[a, :, lanes(k_own)], gc_s.at[a], gc_r.at[a], core)

    def g_pass(a):
        place = gb.at[a, :, lanes(k_side)]
        return remote(place, place, gf_s.at[a], gf_r.at[a], core)

    def x_far(t):
        return remote(x_refs[t], xb.at[t, zl1, bank(x)], xz_s.at[t], xz_r.at[t], far)

    def x_own(t, d):
        return remote(x_refs[t], xb.at[t, zl1, bank(x)], xo_s.at[t, d], xo_r.at[t, d], x_peer[d])

    def x_pass(t, d):
        place = xb.at[t, flip(zl1), bank(x)]
        return remote(place, place, xf_s.at[t, d], xf_r.at[t, d], x_peer[d])

    w_line = 2 * zh + zl0
    home = zl1 == zh

    def w_place(a, k):
        return wb.at[a, k, :, lanes(y)]

    def w_over(a):
        return remote(w_refs[a], w_place(a, zl1), wz_s.at[a, 0], wz_r.at[a, zl1], device(zh_=flip(zh), zl_=w_line))

    def w_here(a):
        return remote(w_refs[a], w_place(a, zl1), wz_s.at[a, 1], wz_r.at[a, zl1], far)

    def w_self(a):
        return pltpu.make_async_copy(w_refs[a], w_place(a, zl1), wz_r.at[a, zl1])

    def w_arrival(a, k):
        return remote(w_place(a, k), w_place(a, k), wz_s.at[a, 0], wz_r.at[a, k], far)

    def w_pass(a, d):
        place = wb.at[a, :, :, lanes(y)]
        return remote(place, place, wy_s.at[a, d], wy_r.at[a, d], y_peer[d])

    def send_w(a):
        start(w_over(a))

        @pl.when(home)
        def _():
            w_self(a).start()

        @pl.when(jnp.logical_not(home))
        def _():
            w_here(a).start()

    def pass_w(a):
        for k in (0, 1):
            w_arrival(a, k).wait_recv()
        for d in near_first:
            start(w_pass(a, d))

    barrier = pltpu.get_barrier_semaphore()
    peers = x_peer + y_peer + [side, far, core, over, over_far]
    for peer in peers:
        pl.semaphore_signal(barrier, inc=1, device_id=peer, device_id_type=MESH)
    pl.semaphore_wait(barrier, len(peers))

    send_w(0)
    for d in near_first:
        start(x_own(1, d))
    start(g_side(ATTN))
    start(g_core(ATTN))
    start(x_far(1))
    for d in near_first:
        start(x_own(0, d))
    send_w(1)
    start(x_far(0))
    send_w(2)
    for a in (0, 1, 2):
        start(g_side(a))
        start(g_core(a))

    def pass_x(t):
        x_far(t).wait_recv()
        for d in near_first:
            start(x_pass(t, d))

    def pass_g(a):
        g_side(a).wait_recv()
        start(g_pass(a))

    def have_x(t):
        own_x(t).wait()
        for d in (0, 1, 2):
            x_own(t, d).wait_recv()
        for d in (0, 1, 2):
            x_pass(t, d).wait_recv()

    def have_g(a):
        own_g(a).wait()
        g_core(a).wait_recv()
        g_pass(a).wait_recv()

    def y_send(a, d):
        to = (y + d + 1) % 4
        if a == ATTN:
            return remote(yso.at[to], yro.at[d], dy_s.at[a, d], dy_r.at[a, d], y_peer[d])
        return remote(ys.at[a, to], yr.at[a, d], dy_s.at[a, d], dy_r.at[a, d], y_peer[d])

    def output_term():
        @pl.loop(0, 4)
        def _(i):
            k, h = i // 2, i % 2
            part = contract_rows(
                gb[ATTN, :, pl.ds(pl.multiple_of(h * 256, 256), 256)], xb[1, k]
            ).astype(BF16)
            columns = pl.ds(pl.multiple_of(k * 512, 512), 512)
            yso[2 * h, :, columns] = part[:128]
            yso[2 * h + 1, :, columns] = part[128:]

        for d in near_first:
            start(y_send(ATTN, d))

    def projection_term(a):
        @pl.loop(0, 4)
        def _(i):
            k, h = i // 2, i % 2
            part = contract_rows(
                xb[0, k, :, pl.ds(pl.multiple_of(h * 256, 256), 256)], gb[a]
            ).astype(BF16)
            rows = pl.ds(pl.multiple_of(i * 256, 256), 256)
            for q in range(4):
                ys[a, q, rows] = part[:, q * 128 : (q + 1) * 128]

        for d in near_first:
            start(y_send(a, d))

    def z_slot(a):
        return zro.at[zh] if a == ATTN else zr.at[a, zh]

    def z_piece(a, k):
        return zso.at[k] if a == ATTN else zs.at[a, k]

    def z_far(a):
        return remote(z_piece(a, flip(zl1)), z_slot(a), dz_s.at[a, 0], dz_r.at[a, zh], device(zh_=zl1, zl_=zl_far))

    def z_over(a):
        return remote(z_piece(a, zl1), z_slot(a), dz_s.at[a, 1], dz_r.at[a, zh], over)

    def z_self(a):
        return pltpu.make_async_copy(z_piece(a, zl1), z_slot(a), dz_r.at[a, zh])

    def z_arrival(a, s):
        place = zro.at[s] if a == ATTN else zr.at[a, s]
        return remote(place, place, dz_s.at[a, 0], dz_r.at[a, s], far)

    def sum_y(a):
        for d in (0, 1, 2):
            y_send(a, d).wait_recv()
        if a == ATTN:
            for k in (0, 1):
                cols = slice(k * 512, (k + 1) * 512)
                total = yso[y, :, cols].astype(F32) + yro[0, :, cols].astype(F32)
                total = total + yro[1, :, cols].astype(F32) + yro[2, :, cols].astype(F32)
                zso[k] = total.astype(BF16)
        else:
            @pl.loop(0, 4)
            def _(i):
                rows = pl.ds(pl.multiple_of(i * 256, 256), 256)
                total = ys[a, y, rows].astype(F32) + yr[a, 0, rows].astype(F32)
                total = total + yr[a, 1, rows].astype(F32) + yr[a, 2, rows].astype(F32)
                zs[a, i // 2, pl.ds(pl.multiple_of((i % 2) * 256, 256), 256)] = total.astype(BF16)

        start(z_far(a))

        @pl.when(home)
        def _():
            z_self(a).start()

        @pl.when(jnp.logical_not(home))
        def _():
            z_over(a).start()

    def gi_part(s):
        return flip(zl1) if s == 0 else zl1

    def gi_send(s, d):
        return remote(xs.at[gi_part(s), (x + d + 1) % 4], xr.at[s, d], gx_s.at[s, d], gx_r.at[s, d], x_peer[d])

    def input_term(s):
        k = gi_part(s)

        @pl.loop(0, 4)
        def _(b):
            rows = bank(b)
            total = contract_columns(gb[0, rows], wb[0, k])
            total = total + contract_columns(gb[1, rows], wb[1, k])
            total = total + contract_columns(gb[2, rows], wb[2, k])
            xs[k, b] = total.astype(BF16)

        for d in near_first:
            start(gi_send(s, d))

    def gi_far():
        return remote(gzs, gz, gg_s, gg_r, far)

    def sum_x(s):
        for d in (0, 1, 2):
            gi_send(s, d).wait_recv()
        total = xs[gi_part(s), x].astype(F32) + xr[s, 0].astype(F32)
        return total + xr[s, 1].astype(F32) + xr[s, 2].astype(F32)

    pass_w(0)
    pass_g(ATTN)
    pass_x(1)
    pass_w(1)
    pass_x(0)
    have_g(ATTN)
    have_x(1)
    output_term()
    pass_w(2)
    pass_g(0)
    have_x(0)
    have_g(0)
    projection_term(0)
    pass_g(1)
    have_g(1)
    projection_term(1)
    sum_y(ATTN)
    pass_g(2)
    have_g(2)
    projection_term(2)
    for a in (0, 1, 2):
        for d in (0, 1, 2):
            w_pass(a, d).wait_recv()
    input_term(0)
    input_term(1)
    sum_y(0)
    sum_y(1)
    gzs[...] = sum_x(0).astype(BF16)
    start(gi_far())
    sum_y(2)
    ownv[...] = sum_x(1)
    own_out = pltpu.make_async_copy(ownv, gown, loc_sem.at[6])
    own_out.start()

    gi_far().wait_recv()
    for a in (ATTN, 0, 1, 2):
        for s in (0, 1):
            z_arrival(a, s).wait_recv()
    own_out.wait()
    for copy in sent:
        copy.wait_send()

    @pl.when(jnp.logical_not(home))
    def _():
        for a in (0, 1, 2):
            w_here(a).wait_send()
        for a in (0, 1, 2, 3):
            z_over(a).wait_send()


def finish_kernel(zr, zro, gz, gown, gi, dq, dk, dv, do):
    for a, out in enumerate((dq, dk, dv)):
        out[...] = zr[a, 0].astype(F32) + zr[a, 1].astype(F32)
    do[...] = zro[0].astype(F32) + zro[1].astype(F32)
    gi[...] = (gown[...] + gz[...].astype(F32)).astype(BF16)


def local(inputs, attn_out, grad_out, grad_query, grad_key, grad_value, query_weight, key_weight, value_weight):
    rows, wide, thin = 256, 512, 128
    sem = pltpu.SemaphoreType.DMA
    vm = pltpu.VMEM
    parts = pl.pallas_call(
        exchange_kernel,
        name="exchange",
        out_shape=(
            jax.ShapeDtypeStruct((3, 2, wide, thin), BF16),
            jax.ShapeDtypeStruct((2, thin, wide), BF16),
            jax.ShapeDtypeStruct((rows, wide), BF16),
            jax.ShapeDtypeStruct((rows, wide), F32),
        ),
        in_specs=[pl.BlockSpec(memory_space=pl.ANY)] * 9,
        out_specs=[pl.BlockSpec(memory_space=pl.ANY)] * 4,
        scratch_shapes=[
            vm((2, 2, 4 * rows, wide), BF16),
            vm((4, 4 * rows, wide), BF16),
            vm((3, 2, wide, wide), BF16),
            vm((3, 4, 2 * wide, thin), BF16),
            vm((4, thin, 2 * wide), BF16),
            vm((3, 3, 2 * wide, thin), BF16),
            vm((3, thin, 2 * wide), BF16),
            vm((3, 2, wide, thin), BF16),
            vm((2, thin, wide), BF16),
            vm((2, 4, rows, wide), BF16),
            vm((2, 3, rows, wide), BF16),
            vm((rows, wide), BF16),
            vm((rows, wide), F32),
            sem((7,)),
            sem((2,)), sem((2,)),
            sem((2, 3)), sem((2, 3)),
            sem((2, 3)), sem((2, 3)),
            sem((4,)), sem((4,)),
            sem((4,)), sem((4,)),
            sem((4,)), sem((4,)),
            sem((3, 2)), sem((3, 2)),
            sem((3, 3)), sem((3, 3)),
            sem((4, 3)), sem((4, 3)),
            sem((4, 2)), sem((4, 2)),
            sem((2, 3)), sem((2, 3)),
            sem, sem,
        ],
        compiler_params=pltpu.CompilerParams(
            collective_id=0, has_side_effects=True, vmem_limit_bytes=56 * 2**20
        ),
    )(
        inputs.reshape(rows, wide),
        grad_out.reshape(rows, wide),
        grad_query.reshape(4 * rows, thin),
        grad_key.reshape(4 * rows, thin),
        grad_value.reshape(4 * rows, thin),
        attn_out.reshape(4 * rows, thin),
        query_weight,
        key_weight,
        value_weight,
    )
    gi, dq, dk, dv, do = pl.pallas_call(
        finish_kernel,
        name="finish",
        out_shape=(
            jax.ShapeDtypeStruct((rows, wide), BF16),
            jax.ShapeDtypeStruct((wide, thin), F32),
            jax.ShapeDtypeStruct((wide, thin), F32),
            jax.ShapeDtypeStruct((wide, thin), F32),
            jax.ShapeDtypeStruct((thin, wide), F32),
        ),
        compiler_params=pltpu.CompilerParams(vmem_limit_bytes=32 * 2**20),
    )(*parts)
    return gi.reshape(inputs.shape), dq, dk, dv, do


def solution(mesh):
    return jax.shard_map(
        local,
        mesh=mesh,
        in_specs=(
            P("ia", "ja", "ka"),
            P(None, "ja", ("ia", "ka")),
            P("ia", "ja", "ka"),
            P(None, "ja", ("ia", "ka")),
            P(None, "ja", ("ia", "ka")),
            P(None, "ja", ("ia", "ka")),
            P("ka", ("ia", "ja")),
            P("ka", ("ia", "ja")),
            P("ka", ("ia", "ja")),
        ),
        out_specs=(
            P("ia", "ja", "ka"),
            P("ka", ("ia", "ja")),
            P("ka", ("ia", "ja")),
            P("ka", ("ia", "ja")),
            P(("ia", "ja"), "ka"),
        ),
        check_vma=False,
    )
```

time: 798 us -> 133 us (0.17)
  waiting for transfers between devices: 742 us -> 0 us
  Pallas kernels: 0 us -> 128 us
  matrix products: 26.6 us -> 0 us
  between operations: 14 us -> 0.65 us
    all_gather x9 -> x0, waiting for transfers between devices: 369 us -> none  [the longest x1 59.7 us: fold_weights(): lax.all_gather(key_weight, 'ja', axis=1, tiled=True)]
    unnamed x17 -> x0, waiting for transfers between devices: 256 us -> none
    pallas_call x0 -> x2, Pallas kernels: none -> 128 us  [the longest x1 126 us: local(): pl.pallas_call(exchange_kernel, name='exchange', out_shape=(jax.ShapeDtyp...]
    reduce_scatter x2 -> x0, waiting for transfers between devices: 116 us -> none  [the longest x1 85.4 us: local(): lax.psum_scatter(output_term.astype(jnp.bfloat16), 'ja', scatter_dimensio...]
    dot_general x7 -> x0, matrix products: 26.6 us -> none  [the longest x3 13.6 us: project(): jnp.einsum('btf,df->btd', grads, weight_piece, preferred_element_type=jnp...]
  transfers between devices with their start and end apart: 14 -> 0, of which waited for: 14 -> 0; matrix products, arithmetic and copies ran while one was open for 5% -> 0% of each run, Pallas kernels for 0% -> 0%
where the time goes in v1:
time: 133 us; the launch traced here: 132 us
  Pallas kernels  128 us (96%)
  local copies, waits for them, and re-layouts  4.07 us (3%)
    pallas_call x1, Pallas kernels, local(): pl.pallas_call(exchange_kernel, name='exchange', out_shape=(jax.ShapeDtyp...  126 us
    unnamed x8, local copies, waits for them, and re-layouts  4.07 us

profile of v1, /device:TPU:1, one launch (start us, length us, event | category | flops | bytes accessed | tf_op | source)
XLA Modules:
  0.0 132.3 jit_solution(14887161065948979650)
XLA Ops:
  0.6 126.4 %exchange.1 = (bf16[3,2,512,128]{3,2,1,0:T(8,128)(2,1)}, bf16[2,128,512]{2,1,0:T(8,128)(2,1)}, bf16[256,512]{1,0:T(8,128)(2,1)}, f32[256,512]{1,0:T(8,128)}) custom-call(bf16[256,512]{1,0:T(8,128)(2,1)} %bitcast.7, bf16[256,512]{1,0:T(8,128)(2,1)} %bitcast.8, bf16[1024,128]{1,0:T(8,128)(2,1)} %bitcast.9, bf16[1024,128]{1,0:T(8,128)(2,1)} %bitcast.10, ...), custom_call_target="tpu_custom_call" | custom-call | tf_op jit(solution)/shard_map/exchange/pallas_call | solution.py:362
  127.1 0.0 copy-start
  127.1 1.1 copy-done
  128.2 0.0 copy-start.1
  128.2 1.0 copy-done.1
  129.3 0.0 copy-start.2
  129.3 0.9 copy-done.2
  130.2 0.0 copy-start.3
  130.2 0.9 copy-done.3
  131.2 1.1 finish.1
Async XLA Ops:
  127.1 1.1 copy-start
  128.2 1.0 copy-start.1
  129.3 0.9 copy-start.2
  130.2 0.9 copy-start.3

commit v2 on v1

v2 whole, which is shorter than its diff:
```python
import functools

import jax
import jax.numpy as jnp
from jax import lax
from jax.experimental import pallas as pl
from jax.experimental.pallas import tpu as pltpu
from jax.sharding import PartitionSpec as P

MESH = pl.DeviceIdType.MESH
BF16 = jnp.bfloat16
F32 = jnp.float32
ATTN = 3


def contract_rows(a, b):
    return lax.dot_general(a, b, (((0,), (0,)), ((), ())), preferred_element_type=F32)


def contract_columns(a, b):
    return lax.dot_general(a, b, (((1,), (1,)), ((), ())), preferred_element_type=F32)


def exchange_kernel(
    in_ref, go_ref, gq_ref, gk_ref, gv_ref, at_ref, wq_ref, wk_ref, wv_ref,
    zr, zro, gz, gown,
    xb, gb, wb, wr, zw, zwo, ys, yso, ya, yao, yr, yro, zs, zso, xs, xa, xr, gzs, ownv,
    loc_sem, xz_s, xz_r, xo_s, xo_r,
    gz_s, gz_r, gc_s, gc_r, gf_s, gf_r,
    wz_s, wz_r, wy_s, wy_r, dy_s, dy_r, dz_s, dz_r,
    gx_s, gx_r, gg_s, gg_r, wr_r, zw_r,
):
    ia, ja, ka = lax.axis_index("ia"), lax.axis_index("ja"), lax.axis_index("ka")
    x, y, zh = ia, ja % 4, ja // 4
    zl, c = ka // 2, ka % 2
    zl1, zl0 = zl // 2, zl % 2

    def device(x_=None, y_=None, zh_=None, zl_=None, c_=None):
        x_ = x if x_ is None else x_
        y_ = y if y_ is None else y_
        zh_ = zh if zh_ is None else zh_
        zl_ = zl if zl_ is None else zl_
        c_ = c if c_ is None else c_
        return (x_, zh_ * 4 + y_, zl_ * 2 + c_)

    def flip(bit):
        return 1 - bit

    def around(i, d):
        return (i + d) % 4

    zl_side = zl1 * 2 + flip(zl0)
    zl_far = flip(zl1) * 2 + zl0
    side, far, core = device(zl_=zl_side), device(zl_=zl_far), device(c_=flip(c))
    over_far = device(zh_=flip(zh), zl_=zl_far)
    x_up, x_down = device(x_=around(x, 1)), device(x_=around(x, 3))
    y_up, y_down = device(y_=around(y, 1)), device(y_=around(y, 3))

    def remote(src, dst, send, recv, to):
        return pltpu.make_async_remote_copy(
            src_ref=src, dst_ref=dst, send_sem=send, recv_sem=recv,
            device_id=to, device_id_type=MESH,
        )

    sent, seen = [], set()

    def start(copy):
        copy.start()
        sent.append(copy)

    def once(key, wait):
        if key not in seen:
            seen.add(key)
            wait()

    def lanes(k):
        return pl.ds(pl.multiple_of(k * 128, 128), 128)

    def bank(b):
        return pl.ds(pl.multiple_of(b * 256, 256), 256)

    g_refs = (gq_ref, gk_ref, gv_ref, at_ref)
    w_refs = (wq_ref, wk_ref, wv_ref)
    x_refs = (in_ref, go_ref)
    k_own, k_side = zl0 * 2 + c, flip(zl0) * 2 + c

    def own_g(a):
        return pltpu.make_async_copy(g_refs[a], gb.at[a, :, lanes(k_own)], loc_sem.at[a])

    def own_x(t):
        return pltpu.make_async_copy(x_refs[t], xb.at[t, zl1, bank(x)], loc_sem.at[4 + t])

    def g_side(a):
        return remote(g_refs[a], gb.at[a, :, lanes(k_own)], gz_s.at[a], gz_r.at[a], side)

    def g_core(a):
        return remote(g_refs[a], gb.at[a, :, lanes(k_own)], gc_s.at[a], gc_r.at[a], core)

    def g_pass(a):
        place = gb.at[a, :, lanes(k_side)]
        return remote(place, place, gf_s.at[a], gf_r.at[a], core)

    def send_g(a):
        start(g_side(a))
        start(g_core(a))

    def pass_g(a):
        g_side(a).wait_recv()
        start(g_pass(a))

    def have_g(a):
        def wait():
            own_g(a).wait()
            g_core(a).wait_recv()
            g_pass(a).wait_recv()

        once(("g", a), wait)

    def x_far(t):
        return remote(x_refs[t], xb.at[t, zl1, bank(x)], xz_s.at[t], xz_r.at[t], far)

    def x_ring(t, j):
        if j < 2:
            src, dst = x_refs[t], xb.at[t, zl1, bank(x)]
        elif j < 4:
            src = dst = xb.at[t, flip(zl1), bank(x)]
        elif j == 4:
            src = dst = xb.at[t, zl1, bank(around(x, 3))]
        else:
            src = dst = xb.at[t, flip(zl1), bank(around(x, 1))]
        return remote(src, dst, xo_s.at[t, j], xo_r.at[t, j], x_down if j % 2 else x_up)

    def send_far(t):
        start(x_far(t))

    def send_x(t):
        start(x_ring(t, 0))
        start(x_ring(t, 1))

    def pass_x(t):
        x_far(t).wait_recv()
        start(x_ring(t, 2))
        start(x_ring(t, 3))

    def forward_own(t):
        x_ring(t, 0).wait_recv()
        start(x_ring(t, 4))

    def forward_far(t):
        x_ring(t, 3).wait_recv()
        start(x_ring(t, 5))

    def have_x(t):
        def wait():
            own_x(t).wait()
            for j in (1, 2, 4, 5):
                x_ring(t, j).wait_recv()

        once(("x", t), wait)

    home = zl1 == zh
    away = jnp.logical_not(home)

    def w_place(a, k):
        return wb.at[a, k, :, lanes(y)]

    def w_first(a, dst, recv):
        return remote(w_refs[a], dst, wz_s.at[a, 0], recv, over_far)

    def w_first_home(a):
        return w_first(a, wr.at[a], wr_r.at[a])

    def w_first_away(a):
        return w_first(a, w_place(a, zl1), wz_r.at[a, zl1])

    def w_second_home(a):
        return remote(wr.at[a], w_place(a, flip(zl1)), wz_s.at[a, 1], wz_r.at[a, flip(zl1)], far)

    def w_second_away(a):
        return remote(w_refs[a], w_place(a, zl1), wz_s.at[a, 1], wz_r.at[a, zl1], far)

    def w_self(a):
        return pltpu.make_async_copy(w_refs[a], w_place(a, zl1), wz_r.at[a, zl1])

    def w_arrival(a, k):
        return remote(w_place(a, k), w_place(a, k), wz_s.at[a, 0], wz_r.at[a, k], far)

    def w_ring(a, j):
        if j < 2:
            place = wb.at[a, :, :, lanes(y)]
        elif j == 2:
            place = wb.at[a, 0, :, lanes(around(y, 3))]
        else:
            place = wb.at[a, 1, :, lanes(around(y, 1))]
        return remote(place, place, wy_s.at[a, j], wy_r.at[a, j], y_down if j % 2 else y_up)

    def send_w(a):
        @pl.when(home)
        def _():
            w_first_home(a).start()
            w_self(a).start()

        @pl.when(away)
        def _():
            w_first_away(a).start()
            w_second_away(a).start()

    def relay_w(a):
        @pl.when(home)
        def _():
            w_first_home(a).wait_recv()
            w_second_home(a).start()

    def pass_w(a):
        for k in (0, 1):
            w_arrival(a, k).wait_recv()
        start(w_ring(a, 0))
        start(w_ring(a, 1))

    def forward_w(a):
        w_ring(a, 0).wait_recv()
        w_ring(a, 1).wait_recv()
        start(w_ring(a, 2))
        start(w_ring(a, 3))

    def have_w(a):
        def wait():
            for j in (2, 3):
                w_ring(a, j).wait_recv()

        once(("w", a), wait)

    def ring_copy(me, up, down, piece, relay, result, send, recv, j):
        if j == 0:
            src, dst = piece(around(me, 2), 0), relay(0)
        elif j == 1:
            src, dst = piece(around(me, 2), 1), relay(1)
        elif j == 2:
            src, dst = piece(around(me, 1), 1), result(0, 1)
        elif j == 3:
            src, dst = piece(around(me, 3), 0), result(1, 0)
        elif j == 4:
            src, dst = piece(around(me, 1), 0), result(0, 0)
        else:
            src, dst = piece(around(me, 3), 1), result(1, 1)
        return remote(src, dst, send(j), recv(j), down if j % 2 else up)

    def ring_add(me, piece, relay):
        for h, d in ((0, 1), (1, 3)):
            place = piece(around(me, d), h)
            place[...] = (place[...].astype(F32) + relay(h)[...].astype(F32)).astype(BF16)

    def ring_total(me, piece, result, h):
        total = piece(me, h)[...].astype(F32) + result(0, h)[...].astype(F32)
        return total + result(1, h)[...].astype(F32)

    def y_piece(a):
        if a == ATTN:
            return lambda q, h: yso.at[q, h]
        return lambda q, h: ys.at[a, q, h]

    def y_relay(a):
        return (lambda h: yao.at[h]) if a == ATTN else (lambda h: ya.at[a, h])

    def y_result(a):
        if a == ATTN:
            return lambda d, h: yro.at[d, h]
        return lambda d, h: yr.at[a, d, h]

    def y_copy(a, j):
        return ring_copy(
            y, y_up, y_down, y_piece(a), y_relay(a), y_result(a),
            lambda i: dy_s.at[a, i], lambda i: dy_r.at[a, i], j,
        )

    def term(a):
        have_x(1 if a == ATTN else 0)
        have_g(a)

        @pl.loop(0, 4)
        def _(i):
            k, h = i // 2, i % 2
            part = pl.ds(pl.multiple_of(h * 256, 256), 256)
            if a == ATTN:
                block = contract_rows(gb[ATTN, :, part], xb[1, k]).astype(BF16)
                yso[2 * h, k] = block[:128]
                yso[2 * h + 1, k] = block[128:]
            else:
                block = contract_rows(xb[0, k, :, part], gb[a]).astype(BF16)
                for q in range(4):
                    ys[a, q, k, part] = block[:, q * 128 : (q + 1) * 128]

        for j in range(4):
            start(y_copy(a, j))

    def combine(a):
        y_copy(a, 0).wait_recv()
        y_copy(a, 1).wait_recv()
        ring_add(y, y_piece(a), y_relay(a))
        start(y_copy(a, 4))
        start(y_copy(a, 5))

    def z_slot(a):
        return zro.at[zh] if a == ATTN else zr.at[a, zh]

    def z_piece(a, k):
        return zso.at[k] if a == ATTN else zs.at[a, k]

    def z_relay(a):
        return zwo if a == ATTN else zw.at[a]

    def z_far_home(a):
        return remote(z_piece(a, flip(zl1)), z_slot(a), dz_s.at[a, 0], dz_r.at[a, zh], far)

    def z_far_away(a):
        return remote(z_piece(a, zl1), z_relay(a), dz_s.at[a, 0], zw_r.at[a], far)

    def z_over_home(a):
        return remote(z_relay(a), z_slot(a), dz_s.at[a, 1], dz_r.at[a, zh], over_far)

    def z_over_away(a):
        return remote(z_piece(a, flip(zl1)), z_slot(a), dz_s.at[a, 1], dz_r.at[a, zh], over_far)

    def z_self(a):
        return pltpu.make_async_copy(z_piece(a, zl1), z_slot(a), dz_r.at[a, zh])

    def z_arrival(a, s):
        place = zro.at[s] if a == ATTN else zr.at[a, s]
        return remote(place, place, dz_s.at[a, 0], dz_r.at[a, s], far)

    def sum_y(a):
        for j in range(2, 6):
            y_copy(a, j).wait_recv()
        for h in (0, 1):
            z_piece(a, h)[...] = ring_total(y, y_piece(a), y_result(a), h).astype(BF16)

        @pl.when(home)
        def _():
            z_far_home(a).start()
            z_self(a).start()

        @pl.when(away)
        def _():
            z_far_away(a).start()
            z_over_away(a).start()

    def relay_z(a):
        @pl.when(home)
        def _():
            z_far_away(a).wait_recv()
            z_over_home(a).start()

    def gi_part(s):
        return flip(zl1) if s == 0 else zl1

    def gi_piece(s):
        return lambda b, h: xs.at[gi_part(s), b, h]

    def gi_copy(s, j):
        return ring_copy(
            x, x_up, x_down, gi_piece(s), lambda h: xa.at[s, h], lambda d, h: xr.at[s, d, h],
            lambda i: gx_s.at[s, i], lambda i: gx_r.at[s, i], j,
        )

    def input_term(s):
        for a in (0, 1, 2):
            have_g(a)
            have_w(a)
        k = gi_part(s)

        @pl.loop(0, 4)
        def _(b):
            rows = bank(b)
            total = contract_columns(gb[0, rows], wb[0, k])
            total = total + contract_columns(gb[1, rows], wb[1, k])
            total = total + contract_columns(gb[2, rows], wb[2, k])
            xs[k, b, 0] = total[:128].astype(BF16)
            xs[k, b, 1] = total[128:].astype(BF16)

        for j in range(4):
            start(gi_copy(s, j))

    def gi_combine(s):
        gi_copy(s, 0).wait_recv()
        gi_copy(s, 1).wait_recv()
        ring_add(x, gi_piece(s), lambda h: xa.at[s, h])
        start(gi_copy(s, 4))
        start(gi_copy(s, 5))

    def gi_far():
        return remote(gzs, gz, gg_s, gg_r, far)

    own_out = pltpu.make_async_copy(ownv, gown, loc_sem.at[6])

    def sum_x(s):
        for j in range(2, 6):
            gi_copy(s, j).wait_recv()
        for h in (0, 1):
            total = ring_total(x, gi_piece(s), lambda d, i: xr.at[s, d, i], h)
            rows = slice(h * 128, (h + 1) * 128)
            if s == 0:
                gzs[rows] = total.astype(BF16)
            else:
                ownv[rows] = total
        if s == 0:
            start(gi_far())
        else:
            own_out.start()

    for a in (0, 1, 2, ATTN):
        own_g(a).start()
    for t in (0, 1):
        own_x(t).start()

    barrier = pltpu.get_barrier_semaphore()
    peers = [x_up, x_down, y_up, y_down, side, far, core, over_far]
    for peer in peers:
        pl.semaphore_signal(barrier, inc=1, device_id=peer, device_id_type=MESH)
    pl.semaphore_wait(barrier, len(peers))

    send_far(0)
    send_w(0)
    send_w(1)
    send_x(1)
    relay_w(0)
    send_x(0)
    send_w(2)
    relay_w(1)
    send_g(0)
    pass_x(0)
    forward_own(1)
    forward_own(0)
    pass_w(0)
    send_g(2)
    relay_w(2)
    pass_w(1)
    send_far(1)
    forward_w(0)
    forward_far(0)
    pass_g(0)
    forward_w(1)
    pass_w(2)
    send_g(1)
    term(0)
    send_g(ATTN)
    pass_x(1)
    pass_g(2)
    forward_w(2)
    combine(0)
    pass_g(1)
    term(1)
    forward_far(1)
    pass_g(ATTN)
    input_term(0)
    input_term(1)
    combine(1)
    sum_y(0)
    term(2)
    combine(2)
    sum_y(1)
    term(ATTN)
    relay_z(0)
    sum_y(2)
    gi_combine(1)
    combine(ATTN)
    relay_z(1)
    gi_combine(0)
    sum_y(ATTN)
    sum_x(1)
    sum_x(0)
    relay_z(2)
    relay_z(ATTN)

    gi_far().wait_recv()
    for a in (0, 1, 2, ATTN):
        for s in (0, 1):
            z_arrival(a, s).wait_recv()
    own_out.wait()
    for copy in sent:
        copy.wait_send()

    @pl.when(home)
    def _():
        for a in (0, 1, 2):
            w_first_home(a).wait_send()
            w_second_home(a).wait_send()
        for a in (0, 1, 2, ATTN):
            z_far_home(a).wait_send()
            z_over_home(a).wait_send()

    @pl.when(away)
    def _():
        for a in (0, 1, 2):
            w_first_away(a).wait_send()
            w_second_away(a).wait_send()
        for a in (0, 1, 2, ATTN):
            z_far_away(a).wait_send()
            z_over_away(a).wait_send()


def finish_kernel(zr_hbm, zro_hbm, gz_hbm, gown_hbm, gi, dq, dk, dv, do, zr, zro, gz, gown, sems):
    pairs = ((zr_hbm, zr), (zro_hbm, zro), (gz_hbm, gz), (gown_hbm, gown))
    copies = [pltpu.make_async_copy(src, dst, sems.at[i]) for i, (src, dst) in enumerate(pairs)]
    for copy in copies:
        copy.start()
    for copy in copies:
        copy.wait()
    for a, out in enumerate((dq, dk, dv)):
        out[...] = zr[a, 0].astype(F32) + zr[a, 1].astype(F32)
    do[...] = zro[0].astype(F32) + zro[1].astype(F32)
    gi[...] = (gown[...] + gz[...].astype(F32)).astype(BF16)


def local(inputs, attn_out, grad_out, grad_query, grad_key, grad_value, query_weight, key_weight, value_weight):
    rows, wide, thin = 256, 512, 128
    sem = pltpu.SemaphoreType.DMA
    vm = pltpu.VMEM
    parts = pl.pallas_call(
        exchange_kernel,
        name="exchange",
        out_shape=(
            jax.ShapeDtypeStruct((3, 2, wide, thin), BF16),
            jax.ShapeDtypeStruct((2, thin, wide), BF16),
            jax.ShapeDtypeStruct((rows, wide), BF16),
            jax.ShapeDtypeStruct((rows, wide), F32),
        ),
        in_specs=[pl.BlockSpec(memory_space=pl.ANY)] * 9,
        out_specs=[pl.BlockSpec(memory_space=pl.ANY)] * 4,
        scratch_shapes=[
            vm((2, 2, 4 * rows, wide), BF16),
            vm((4, 4 * rows, wide), BF16),
            vm((3, 2, wide, wide), BF16),
            vm((3, wide, thin), BF16),
            vm((3, wide, thin), BF16),
            vm((thin, wide), BF16),
            vm((3, 4, 2, wide, thin), BF16),
            vm((4, 2, thin, wide), BF16),
            vm((3, 2, wide, thin), BF16),
            vm((2, thin, wide), BF16),
            vm((3, 2, 2, wide, thin), BF16),
            vm((2, 2, thin, wide), BF16),
            vm((3, 2, wide, thin), BF16),
            vm((2, thin, wide), BF16),
            vm((2, 4, 2, thin, wide), BF16),
            vm((2, 2, thin, wide), BF16),
            vm((2, 2, 2, thin, wide), BF16),
            vm((rows, wide), BF16),
            vm((rows, wide), F32),
            sem((7,)),
            sem((2,)), sem((2,)),
            sem((2, 6)), sem((2, 6)),
            sem((4,)), sem((4,)),
            sem((4,)), sem((4,)),
            sem((4,)), sem((4,)),
            sem((3, 2)), sem((3, 2)),
            sem((3, 4)), sem((3, 4)),
            sem((4, 6)), sem((4, 6)),
            sem((4, 2)), sem((4, 2)),
            sem((2, 6)), sem((2, 6)),
            sem, sem,
            sem((3,)), sem((4,)),
        ],
        compiler_params=pltpu.CompilerParams(
            collective_id=0, has_side_effects=True, vmem_limit_bytes=56 * 2**20
        ),
    )(
        inputs.reshape(rows, wide),
        grad_out.reshape(rows, wide),
        grad_query.reshape(4 * rows, thin),
        grad_key.reshape(4 * rows, thin),
        grad_value.reshape(4 * rows, thin),
        attn_out.reshape(4 * rows, thin),
        query_weight,
        key_weight,
        value_weight,
    )
    gi, dq, dk, dv, do = pl.pallas_call(
        finish_kernel,
        name="finish",
        out_shape=(
            jax.ShapeDtypeStruct((rows, wide), BF16),
            jax.ShapeDtypeStruct((wide, thin), F32),
            jax.ShapeDtypeStruct((wide, thin), F32),
            jax.ShapeDtypeStruct((wide, thin), F32),
            jax.ShapeDtypeStruct((thin, wide), F32),
        ),
        in_specs=[pl.BlockSpec(memory_space=pl.ANY)] * 4,
        scratch_shapes=[
            vm((3, 2, wide, thin), BF16),
            vm((2, thin, wide), BF16),
            vm((rows, wide), BF16),
            vm((rows, wide), F32),
            sem((4,)),
        ],
        compiler_params=pltpu.CompilerParams(vmem_limit_bytes=62 * 2**20),
    )(*parts)
    return gi.reshape(inputs.shape), dq, dk, dv, do


def solution(mesh):
    return jax.shard_map(
        local,
        mesh=mesh,
        in_specs=(
            P("ia", "ja", "ka"),
            P(None, "ja", ("ia", "ka")),
            P("ia", "ja", "ka"),
            P(None, "ja", ("ia", "ka")),
            P(None, "ja", ("ia", "ka")),
            P(None, "ja", ("ia", "ka")),
            P("ka", ("ia", "ja")),
            P("ka", ("ia", "ja")),
            P("ka", ("ia", "ja")),
        ),
        out_specs=(
            P("ia", "ja", "ka"),
            P("ka", ("ia", "ja")),
            P("ka", ("ia", "ja")),
            P("ka", ("ia", "ja")),
            P(("ia", "ja"), "ka"),
        ),
        check_vma=False,
    )
```

time: 133 us -> 112 us (0.84)
  Pallas kernels: 128 us -> 110 us
  local copies, waits for them, and re-layouts: 4.07 us -> 0 us
    pallas_call x1, Pallas kernels: 126 us -> 108 us  [local(): pl.pallas_call(exchange_kernel, name='exchange', out_shape=(jax.ShapeDtyp...]
    unnamed x8 -> x0, local copies, waits for them, and re-layouts: 4.07 us -> none
    pallas_call x1, Pallas kernels: 1.13 us -> 2.55 us  [local(): pl.pallas_call(finish_kernel, name='finish', out_shape=(jax.ShapeDtypeStr...]
where the time goes in v2:
time: 112 us; the launch traced here: 111 us
  Pallas kernels  110 us (98%)
    pallas_call x1, Pallas kernels, local(): pl.pallas_call(exchange_kernel, name='exchange', out_shape=(jax.ShapeDtyp...  108 us
    pallas_call x1, Pallas kernels, local(): pl.pallas_call(finish_kernel, name='finish', out_shape=(jax.ShapeDtypeStr...  2.55 us

profile of v2, /device:TPU:1, one launch (start us, length us, event | category | flops | bytes accessed | tf_op | source)
XLA Modules:
  0.0 111.1 jit_solution(10890240526225070013)
XLA Ops:
  0.6 107.9 %exchange.1 = (bf16[3,2,512,128]{3,2,1,0:T(8,128)(2,1)}, bf16[2,128,512]{2,1,0:T(8,128)(2,1)}, bf16[256,512]{1,0:T(8,128)(2,1)}, f32[256,512]{1,0:T(8,128)}) custom-call(bf16[256,512]{1,0:T(8,128)(2,1)} %bitcast.7, bf16[256,512]{1,0:T(8,128)(2,1)} %bitcast.8, bf16[1024,128]{1,0:T(8,128)(2,1)} %bitcast.9, bf16[1024,128]{1,0:T(8,128)(2,1)} %bitcast.10, ...), custom_call_target="tpu_custom_call" | custom-call | tf_op jit(solution)/shard_map/exchange/pallas_call | solution.py:518
  108.6 2.5 %finish.1 = (bf16[256,512]{1,0:T(8,128)(2,1)}, f32[512,128]{1,0:T(8,128)}, f32[512,128]{1,0:T(8,128)}, f32[512,128]{1,0:T(8,128)}, f32[128,512]{1,0:T(8,128)}) custom-call(bf16[3,2,512,128]{3,2,1,0:T(8,128)(2,1)} %get-tuple-element.14.zr_hbm, bf16[2,128,512]{2,1,0:T(8,128)(2,1)} %get-tuple-element.15.zro_hbm, bf16[256,512]{1,0:T(8,128)(2,1)} %get-tuple-element.16.gz_hbm, ...), custom_call_target="tpu_custom_call" | custom-call | tf_op jit(solution)/shard_map/finish/pallas_call | solution.py:577

commit v3 on v2

--- a/solution.py
+++ b/solution.py
@@ -187,11 +187,13 @@
 
     def w_ring(a, j):
         if j < 2:
-            place = wb.at[a, :, :, lanes(y)]
-        elif j == 2:
-            place = wb.at[a, 0, :, lanes(around(y, 3))]
+            place = wb.at[a, zh, :, lanes(y)]
+        elif j < 4:
+            place = wb.at[a, flip(zh), :, lanes(y)]
+        elif j == 4:
+            place = wb.at[a, zh, :, lanes(around(y, 3))]
         else:
-            place = wb.at[a, 1, :, lanes(around(y, 1))]
+            place = wb.at[a, flip(zh), :, lanes(around(y, 1))]
         return remote(place, place, wy_s.at[a, j], wy_r.at[a, j], y_down if j % 2 else y_up)
 
     def send_w(a):
@@ -211,21 +213,27 @@
             w_first_home(a).wait_recv()
             w_second_home(a).start()
 
-    def pass_w(a):
-        for k in (0, 1):
-            w_arrival(a, k).wait_recv()
+    def pass_first(a):
+        w_arrival(a, zh).wait_recv()
         start(w_ring(a, 0))
         start(w_ring(a, 1))
 
-    def forward_w(a):
-        w_ring(a, 0).wait_recv()
-        w_ring(a, 1).wait_recv()
+    def pass_second(a):
+        w_arrival(a, flip(zh)).wait_recv()
         start(w_ring(a, 2))
         start(w_ring(a, 3))
 
+    def forward_first(a):
+        w_ring(a, 0).wait_recv()
+        start(w_ring(a, 4))
+
+    def forward_second(a):
+        w_ring(a, 3).wait_recv()
+        start(w_ring(a, 5))
+
     def have_w(a):
         def wait():
-            for j in (2, 3):
+            for j in (1, 2, 4, 5):
                 w_ring(a, j).wait_recv()
 
         once(("w", a), wait)
@@ -254,101 +262,108 @@
         total = piece(me, h)[...].astype(F32) + result(0, h)[...].astype(F32)
         return total + result(1, h)[...].astype(F32)
 
-    def y_piece(a):
+    def y_piece(a, s):
         if a == ATTN:
-            return lambda q, h: yso.at[q, h]
-        return lambda q, h: ys.at[a, q, h]
-
-    def y_relay(a):
-        return (lambda h: yao.at[h]) if a == ATTN else (lambda h: ya.at[a, h])
-
-    def y_result(a):
+            return lambda q, h: yso.at[q, s, h]
+        return lambda q, h: ys.at[a, q, s, h]
+
+    def y_relay(a, s):
+        return (lambda h: yao.at[s, h]) if a == ATTN else (lambda h: ya.at[a, s, h])
+
+    def y_result(a, s):
         if a == ATTN:
-            return lambda d, h: yro.at[d, h]
-        return lambda d, h: yr.at[a, d, h]
-
-    def y_copy(a, j):
+            return lambda d, h: yro.at[s, d, h]
+        return lambda d, h: yr.at[a, s, d, h]
+
+    def y_copy(a, s, j):
         return ring_copy(
-            y, y_up, y_down, y_piece(a), y_relay(a), y_result(a),
-            lambda i: dy_s.at[a, i], lambda i: dy_r.at[a, i], j,
+            y, y_up, y_down, y_piece(a, s), y_relay(a, s), y_result(a, s),
+            lambda i: dy_s.at[a * 2 + s, i], lambda i: dy_r.at[a * 2 + s, i], j,
         )
 
-    def term(a):
+    def term(a, s):
         have_x(1 if a == ATTN else 0)
         have_g(a)
-
-        @pl.loop(0, 4)
-        def _(i):
-            k, h = i // 2, i % 2
-            part = pl.ds(pl.multiple_of(h * 256, 256), 256)
+        part = slice(s * 256, (s + 1) * 256)
+
+        @pl.loop(0, 2)
+        def _(k):
             if a == ATTN:
-                block = contract_rows(gb[ATTN, :, part], xb[1, k]).astype(BF16)
-                yso[2 * h, k] = block[:128]
-                yso[2 * h + 1, k] = block[128:]
+                block = contract_rows(gb[ATTN], xb[1, k, :, part]).astype(BF16)
+                for q in range(4):
+                    yso[q, s, k] = block[q * 128 : (q + 1) * 128]
             else:
                 block = contract_rows(xb[0, k, :, part], gb[a]).astype(BF16)
                 for q in range(4):
-                    ys[a, q, k, part] = block[:, q * 128 : (q + 1) * 128]
+                    ys[a, q, s, k] = block[:, q * 128 : (q + 1) * 128]
 
         for j in range(4):
-            start(y_copy(a, j))
-
-    def combine(a):
-        y_copy(a, 0).wait_recv()
-        y_copy(a, 1).wait_recv()
-        ring_add(y, y_piece(a), y_relay(a))
-        start(y_copy(a, 4))
-        start(y_copy(a, 5))
-
-    def z_slot(a):
-        return zro.at[zh] if a == ATTN else zr.at[a, zh]
-
-    def z_piece(a, k):
-        return zso.at[k] if a == ATTN else zs.at[a, k]
-
-    def z_relay(a):
-        return zwo if a == ATTN else zw.at[a]
-
-    def z_far_home(a):
-        return remote(z_piece(a, flip(zl1)), z_slot(a), dz_s.at[a, 0], dz_r.at[a, zh], far)
-
-    def z_far_away(a):
-        return remote(z_piece(a, zl1), z_relay(a), dz_s.at[a, 0], zw_r.at[a], far)
-
-    def z_over_home(a):
-        return remote(z_relay(a), z_slot(a), dz_s.at[a, 1], dz_r.at[a, zh], over_far)
-
-    def z_over_away(a):
-        return remote(z_piece(a, flip(zl1)), z_slot(a), dz_s.at[a, 1], dz_r.at[a, zh], over_far)
-
-    def z_self(a):
-        return pltpu.make_async_copy(z_piece(a, zl1), z_slot(a), dz_r.at[a, zh])
-
-    def z_arrival(a, s):
-        place = zro.at[s] if a == ATTN else zr.at[a, s]
-        return remote(place, place, dz_s.at[a, 0], dz_r.at[a, s], far)
-
-    def sum_y(a):
+            start(y_copy(a, s, j))
+
+    def combine(a, s):
+        y_copy(a, s, 0).wait_recv()
+        y_copy(a, s, 1).wait_recv()
+        ring_add(y, y_piece(a, s), y_relay(a, s))
+        start(y_copy(a, s, 4))
+        start(y_copy(a, s, 5))
+
+    def z_place(a, s, slot):
+        part = pl.ds(s * 256, 256)
+        return zro.at[slot, :, part] if a == ATTN else zr.at[a, slot, part]
+
+    def z_piece(a, s, k):
+        return zso.at[s, k] if a == ATTN else zs.at[a, s, k]
+
+    def z_relay(a, s):
+        return zwo.at[s] if a == ATTN else zw.at[a, s]
+
+    def z_copy(a, s, i, src, dst, recv, to):
+        return remote(src, dst, dz_s.at[a * 2 + s, i], recv, to)
+
+    def z_sem(a, s):
+        return dz_r.at[a * 2 + s, zh]
+
+    def z_far_home(a, s):
+        return z_copy(a, s, 0, z_piece(a, s, flip(zl1)), z_place(a, s, zh), z_sem(a, s), far)
+
+    def z_far_away(a, s):
+        return z_copy(a, s, 0, z_piece(a, s, zl1), z_relay(a, s), zw_r.at[a * 2 + s], far)
+
+    def z_over_home(a, s):
+        return z_copy(a, s, 1, z_relay(a, s), z_place(a, s, zh), z_sem(a, s), over_far)
+
+    def z_over_away(a, s):
+        return z_copy(a, s, 1, z_piece(a, s, flip(zl1)), z_place(a, s, zh), z_sem(a, s), over_far)
+
+    def z_self(a, s):
+        return pltpu.make_async_copy(z_piece(a, s, zl1), z_place(a, s, zh), z_sem(a, s))
+
+    def z_arrival(a, s, slot):
+        place = z_place(a, s, slot)
+        return remote(place, place, dz_s.at[a * 2 + s, 0], dz_r.at[a * 2 + s, slot], far)
+
+    def sum_y(a, s):
         for j in range(2, 6):
-            y_copy(a, j).wait_recv()
+            y_copy(a, s, j).wait_recv()
         for h in (0, 1):
-            z_piece(a, h)[...] = ring_total(y, y_piece(a), y_result(a), h).astype(BF16)
+            total = ring_total(y, y_piece(a, s), y_result(a, s), h)
+            z_piece(a, s, h)[...] = total.astype(BF16)
 
         @pl.when(home)
         def _():
-            z_far_home(a).start()
-            z_self(a).start()
+            z_far_home(a, s).start()
+            z_self(a, s).start()
 
         @pl.when(away)
         def _():
-            z_far_away(a).start()
-            z_over_away(a).start()
-
-    def relay_z(a):
+            z_far_away(a, s).start()
+            z_over_away(a, s).start()
+
+    def relay_z(a, s):
         @pl.when(home)
         def _():
-            z_far_away(a).wait_recv()
-            z_over_home(a).start()
+            z_far_away(a, s).wait_recv()
+            z_over_home(a, s).start()
 
     def gi_part(s):
         return flip(zl1) if s == 0 else zl1
@@ -419,62 +434,85 @@
     pl.semaphore_wait(barrier, len(peers))
 
     send_far(0)
+    send_w(2)
+    send_x(0)
     send_w(0)
     send_w(1)
+    relay_w(2)
+    relay_w(0)
+    pass_first(2)
+    pass_x(0)
+    forward_own(0)
+    pass_first(0)
+    relay_w(1)
     send_x(1)
-    relay_w(0)
-    send_x(0)
-    send_w(2)
-    relay_w(1)
+    pass_second(2)
+    pass_first(1)
+    send_g(2)
+    send_g(1)
+    send_far(1)
+    forward_far(0)
+    forward_first(2)
+    pass_second(0)
+    forward_first(1)
+    forward_first(0)
+    forward_second(2)
+    pass_second(1)
     send_g(0)
-    pass_x(0)
+    forward_second(0)
     forward_own(1)
-    forward_own(0)
-    pass_w(0)
-    send_g(2)
-    relay_w(2)
-    pass_w(1)
-    send_far(1)
-    forward_w(0)
-    forward_far(0)
+    pass_g(2)
+    send_g(ATTN)
+    forward_second(1)
+    term(2, 0)
+    term(2, 1)
+    pass_g(1)
+    combine(2, 1)
+    term(1, 1)
+    pass_x(1)
+    combine(2, 0)
+    term(1, 0)
     pass_g(0)
-    forward_w(1)
-    pass_w(2)
-    send_g(1)
-    term(0)
-    send_g(ATTN)
-    pass_x(1)
-    pass_g(2)
-    forward_w(2)
-    combine(0)
-    pass_g(1)
-    term(1)
+    combine(1, 1)
+    combine(1, 0)
+    sum_y(2, 1)
     forward_far(1)
+    sum_y(2, 0)
+    term(0, 1)
+    sum_y(1, 1)
+    term(0, 0)
     pass_g(ATTN)
+    combine(0, 1)
     input_term(0)
+    combine(0, 0)
+    term(ATTN, 0)
+    sum_y(1, 0)
+    relay_z(1, 1)
+    relay_z(2, 0)
+    term(ATTN, 1)
+    sum_y(0, 0)
+    gi_combine(0)
+    relay_z(2, 1)
+    sum_y(0, 1)
+    combine(ATTN, 0)
     input_term(1)
-    combine(1)
-    sum_y(0)
-    term(2)
-    combine(2)
-    sum_y(1)
-    term(ATTN)
-    relay_z(0)
-    sum_y(2)
+    combine(ATTN, 1)
+    sum_y(ATTN, 0)
+    relay_z(0, 0)
+    sum_y(ATTN, 1)
     gi_combine(1)
-    combine(ATTN)
-    relay_z(1)
-    gi_combine(0)
-    sum_y(ATTN)
+    relay_z(0, 1)
+    sum_x(0)
+    relay_z(ATTN, 0)
+    relay_z(1, 0)
+    relay_z(ATTN, 1)
     sum_x(1)
-    sum_x(0)
-    relay_z(2)
-    relay_z(ATTN)
 
     gi_far().wait_recv()
     for a in (0, 1, 2, ATTN):
         for s in (0, 1):
-            z_arrival(a, s).wait_recv()
+            for slot in (0, 1):
+                z_arrival(a, s, slot).wait_recv()
     own_out.wait()
     for copy in sent:
         copy.wait_send()
@@ -485,8 +523,9 @@
             w_first_home(a).wait_send()
             w_second_home(a).wait_send()
         for a in (0, 1, 2, ATTN):
-            z_far_home(a).wait_send()
-            z_over_home(a).wait_send()
+            for s in (0, 1):
+                z_far_home(a, s).wait_send()
+                z_over_home(a, s).wait_send()
 
     @pl.when(away)
     def _():
@@ -494,8 +533,9 @@
             w_first_away(a).wait_send()
             w_second_away(a).wait_send()
         for a in (0, 1, 2, ATTN):
-            z_far_away(a).wait_send()
-            z_over_away(a).wait_send()
+            for s in (0, 1):
+                z_far_away(a, s).wait_send()
+                z_over_away(a, s).wait_send()
 
 
 def finish_kernel(zr_hbm, zro_hbm, gz_hbm, gown_hbm, gi, dq, dk, dv, do, zr, zro, gz, gown, sems):
@@ -531,16 +571,16 @@
             vm((4, 4 * rows, wide), BF16),
             vm((3, 2, wide, wide), BF16),
             vm((3, wide, thin), BF16),
-            vm((3, wide, thin), BF16),
-            vm((thin, wide), BF16),
-            vm((3, 4, 2, wide, thin), BF16),
-            vm((4, 2, thin, wide), BF16),
-            vm((3, 2, wide, thin), BF16),
-            vm((2, thin, wide), BF16),
-            vm((3, 2, 2, wide, thin), BF16),
-            vm((2, 2, thin, wide), BF16),
-            vm((3, 2, wide, thin), BF16),
-            vm((2, thin, wide), BF16),
+            vm((3, 2, rows, thin), BF16),
+            vm((2, thin, rows), BF16),
+            vm((3, 4, 2, 2, rows, thin), BF16),
+            vm((4, 2, 2, thin, rows), BF16),
+            vm((3, 2, 2, rows, thin), BF16),
+            vm((2, 2, thin, rows), BF16),
+            vm((3, 2, 2, 2, rows, thin), BF16),
+            vm((2, 2, 2, thin, rows), BF16),
+            vm((3, 2, 2, rows, thin), BF16),
+            vm((2, 2, thin, rows), BF16),
             vm((2, 4, 2, thin, wide), BF16),
             vm((2, 2, thin, wide), BF16),
             vm((2, 2, 2, thin, wide), BF16),
@@ -553,12 +593,12 @@
             sem((4,)), sem((4,)),
             sem((4,)), sem((4,)),
             sem((3, 2)), sem((3, 2)),
-            sem((3, 4)), sem((3, 4)),
-            sem((4, 6)), sem((4, 6)),
-            sem((4, 2)), sem((4, 2)),
+            sem((3, 6)), sem((3, 6)),
+            sem((8, 6)), sem((8, 6)),
+            sem((8, 2)), sem((8, 2)),
             sem((2, 6)), sem((2, 6)),
             sem, sem,
-            sem((3,)), sem((4,)),
+            sem((3,)), sem((8,)),
         ],
         compiler_params=pltpu.CompilerParams(
             collective_id=0, has_side_effects=True, vmem_limit_bytes=56 * 2**20

time: 112 us -> 107 us (0.955)
  the two profiles are of different devices: /device:TPU:1 before, /device:TPU:64 now
where the time goes in v3:
time: 107 us
  Pallas kernels  106 us (99%)
    pallas_call x1, Pallas kernels, local(): pl.pallas_call(exchange_kernel, name='exchange', out_shape=(jax.ShapeDtyp...  104 us
    pallas_call x1, Pallas kernels, local(): pl.pallas_call(finish_kernel, name='finish', out_shape=(jax.ShapeDtypeStr...  2.55 us

profile of v3, /device:TPU:64, one launch (start us, length us, event | category | flops | bytes accessed | tf_op | source)
XLA Modules:
  0.0 107.1 jit_solution(16885755005838568153)
XLA Ops:
  0.6 103.9 %exchange.1 = (bf16[3,2,512,128]{3,2,1,0:T(8,128)(2,1)}, bf16[2,128,512]{2,1,0:T(8,128)(2,1)}, bf16[256,512]{1,0:T(8,128)(2,1)}, f32[256,512]{1,0:T(8,128)}) custom-call(bf16[256,512]{1,0:T(8,128)(2,1)} %bitcast.7, bf16[256,512]{1,0:T(8,128)(2,1)} %bitcast.8, bf16[1024,128]{1,0:T(8,128)(2,1)} %bitcast.9, bf16[1024,128]{1,0:T(8,128)(2,1)} %bitcast.10, ...), custom_call_target="tpu_custom_call" | custom-call | tf_op jit(solution)/shard_map/exchange/pallas_call | solution.py:558
  104.5 2.5 %finish.1 = (bf16[256,512]{1,0:T(8,128)(2,1)}, f32[512,128]{1,0:T(8,128)}, f32[512,128]{1,0:T(8,128)}, f32[512,128]{1,0:T(8,128)}, f32[128,512]{1,0:T(8,128)}) custom-call(bf16[3,2,512,128]{3,2,1,0:T(8,128)(2,1)} %get-tuple-element.14.zr_hbm, bf16[2,128,512]{2,1,0:T(8,128)(2,1)} %get-tuple-element.15.zro_hbm, bf16[256,512]{1,0:T(8,128)(2,1)} %get-tuple-element.16.gz_hbm, ...), custom_call_target="tpu_custom_call" | custom-call | tf_op jit(solution)/shard_map/finish/pallas_call | solution.py:617

commit v4 on v3

--- a/solution.py
+++ b/solution.py
@@ -435,77 +435,77 @@
 
     send_far(0)
     send_w(2)
-    send_x(0)
     send_w(0)
     send_w(1)
     relay_w(2)
+    pass_first(2)
+    send_x(0)
+    pass_x(0)
+    pass_first(0)
     relay_w(0)
-    pass_first(2)
-    pass_x(0)
-    forward_own(0)
-    pass_first(0)
-    relay_w(1)
     send_x(1)
     pass_second(2)
     pass_first(1)
+    relay_w(1)
+    send_g(1)
+    send_g(0)
+    forward_far(0)
+    forward_first(0)
+    pass_second(0)
+    forward_own(0)
+    forward_second(2)
+    forward_first(1)
+    send_far(1)
+    pass_second(1)
+    forward_second(0)
+    pass_g(1)
+    forward_second(1)
+    forward_first(2)
+    term(1, 0)
+    term(1, 1)
+    pass_g(0)
+    forward_own(1)
     send_g(2)
-    send_g(1)
-    send_far(1)
-    forward_far(0)
-    forward_first(2)
-    pass_second(0)
-    forward_first(1)
-    forward_first(0)
-    forward_second(2)
-    pass_second(1)
-    send_g(0)
-    forward_second(0)
-    forward_own(1)
+    combine(1, 0)
+    pass_x(1)
+    term(0, 0)
+    send_g(ATTN)
+    term(0, 1)
     pass_g(2)
-    send_g(ATTN)
-    forward_second(1)
+    combine(1, 1)
+    combine(0, 0)
+    sum_y(1, 0)
+    forward_far(1)
+    combine(0, 1)
+    term(2, 1)
+    pass_g(ATTN)
     term(2, 0)
-    term(2, 1)
-    pass_g(1)
+    sum_y(0, 0)
+    sum_y(1, 1)
+    sum_y(0, 1)
     combine(2, 1)
-    term(1, 1)
-    pass_x(1)
+    term(ATTN, 0)
+    relay_z(1, 0)
+    input_term(0)
     combine(2, 0)
-    term(1, 0)
-    pass_g(0)
-    combine(1, 1)
-    combine(1, 0)
     sum_y(2, 1)
-    forward_far(1)
+    combine(ATTN, 0)
+    term(ATTN, 1)
+    relay_z(1, 1)
     sum_y(2, 0)
-    term(0, 1)
-    sum_y(1, 1)
-    term(0, 0)
-    pass_g(ATTN)
-    combine(0, 1)
-    input_term(0)
-    combine(0, 0)
-    term(ATTN, 0)
-    sum_y(1, 0)
-    relay_z(1, 1)
+    relay_z(0, 0)
+    sum_y(ATTN, 0)
+    relay_z(0, 1)
+    gi_combine(0)
+    combine(ATTN, 1)
+    sum_y(ATTN, 1)
     relay_z(2, 0)
-    term(ATTN, 1)
-    sum_y(0, 0)
-    gi_combine(0)
+    sum_x(0)
     relay_z(2, 1)
-    sum_y(0, 1)
-    combine(ATTN, 0)
     input_term(1)
-    combine(ATTN, 1)
-    sum_y(ATTN, 0)
-    relay_z(0, 0)
-    sum_y(ATTN, 1)
+    relay_z(ATTN, 0)
+    relay_z(ATTN, 1)
     gi_combine(1)
-    relay_z(0, 1)
-    sum_x(0)
-    relay_z(ATTN, 0)
-    relay_z(1, 0)
-    relay_z(ATTN, 1)
     sum_x(1)
 
     gi_far().wait_recv()
@@ -538,17 +538,28 @@
                 z_over_away(a, s).wait_send()
 
 
-def finish_kernel(zr_hbm, zro_hbm, gz_hbm, gown_hbm, gi, dq, dk, dv, do, zr, zro, gz, gown, sems):
-    pairs = ((zr_hbm, zr), (zro_hbm, zro), (gz_hbm, gz), (gown_hbm, gown))
-    copies = [pltpu.make_async_copy(src, dst, sems.at[i]) for i, (src, dst) in enumerate(pairs)]
-    for copy in copies:
+def finish_kernel(zr_hbm, zro_hbm, gz_hbm, gown_hbm, gi, dq, dk, dv, do, zr, zro, gz, gown, gi_v, dw_v, do_v, sems):
+    moves = [(zr_hbm.at[a], zr.at[a]) for a in (0, 1, 2)]
+    moves += [(zro_hbm, zro), (gz_hbm, gz), (gown_hbm, gown)]
+    loads = [pltpu.make_async_copy(src, dst, sems.at[i]) for i, (src, dst) in enumerate(moves)]
+    places = [(dw_v.at[a], out) for a, out in enumerate((dq, dk, dv))]
+    places += [(do_v, do), (gi_v, gi)]
+    stores = [pltpu.make_async_copy(src, dst, sems.at[6 + i]) for i, (src, dst) in enumerate(places)]
+    for copy in loads:
         copy.start()
-    for copy in copies:
+    for a in (0, 1, 2):
+        loads[a].wait()
+        dw_v[a] = zr[a, 0].astype(F32) + zr[a, 1].astype(F32)
+        stores[a].start()
+    loads[3].wait()
+    do_v[...] = zro[0].astype(F32) + zro[1].astype(F32)
+    stores[3].start()
+    loads[4].wait()
+    loads[5].wait()
+    gi_v[...] = (gown[...] + gz[...].astype(F32)).astype(BF16)
+    stores[4].start()
+    for copy in stores:
         copy.wait()
-    for a, out in enumerate((dq, dk, dv)):
-        out[...] = zr[a, 0].astype(F32) + zr[a, 1].astype(F32)
-    do[...] = zro[0].astype(F32) + zro[1].astype(F32)
-    gi[...] = (gown[...] + gz[...].astype(F32)).astype(BF16)
 
 
 def local(inputs, attn_out, grad_out, grad_query, grad_key, grad_value, query_weight, key_weight, value_weight):
@@ -625,12 +636,16 @@
             jax.ShapeDtypeStruct((thin, wide), F32),
         ),
         in_specs=[pl.BlockSpec(memory_space=pl.ANY)] * 4,
+        out_specs=[pl.BlockSpec(memory_space=pl.ANY)] * 5,
         scratch_shapes=[
             vm((3, 2, wide, thin), BF16),
             vm((2, thin, wide), BF16),
             vm((rows, wide), BF16),
             vm((rows, wide), F32),
-            sem((4,)),
+            vm((rows, wide), BF16),
+            vm((3, wide, thin), F32),
+            vm((thin, wide), F32),
+            sem((11,)),
         ],
         compiler_params=pltpu.CompilerParams(vmem_limit_bytes=62 * 2**20),
     )(*parts)

time: 107 us -> 107 us (level)
  the two profiles are of different devices: /device:TPU:64 before, /device:TPU:1 now
where the time goes in v4:
time: 107 us
  Pallas kernels  106 us (99%)
    pallas_call x1, Pallas kernels, local(): pl.pallas_call(exchange_kernel, name='exchange', out_shape=(jax.ShapeDtyp...  104 us
    pallas_call x1, Pallas kernels, local(): pl.pallas_call(finish_kernel, name='finish', out_shape=(jax.ShapeDtypeStr...  2.29 us

profile of v4, /device:TPU:1, one launch (start us, length us, event | category | flops | bytes accessed | tf_op | source)
XLA Modules:
  0.0 106.6 jit_solution(2266655757203684873)
XLA Ops:
  0.6 103.7 %exchange.1 = (bf16[3,2,512,128]{3,2,1,0:T(8,128)(2,1)}, bf16[2,128,512]{2,1,0:T(8,128)(2,1)}, bf16[256,512]{1,0:T(8,128)(2,1)}, f32[256,512]{1,0:T(8,128)}) custom-call(bf16[256,512]{1,0:T(8,128)(2,1)} %bitcast.7, bf16[256,512]{1,0:T(8,128)(2,1)} %bitcast.8, bf16[1024,128]{1,0:T(8,128)(2,1)} %bitcast.9, bf16[1024,128]{1,0:T(8,128)(2,1)} %bitcast.10, ...), custom_call_target="tpu_custom_call" | custom-call | tf_op jit(solution)/shard_map/exchange/pallas_call | solution.py:569
  104.4 2.3 %finish.1 = (bf16[256,512]{1,0:T(8,128)(2,1)}, f32[512,128]{1,0:T(8,128)}, f32[512,128]{1,0:T(8,128)}, f32[512,128]{1,0:T(8,128)}, f32[128,512]{1,0:T(8,128)}) custom-call(bf16[3,2,512,128]{3,2,1,0:T(8,128)(2,1)} %get-tuple-element.14.zr_hbm, bf16[2,128,512]{2,1,0:T(8,128)(2,1)} %get-tuple-element.15.zro_hbm, bf16[256,512]{1,0:T(8,128)(2,1)} %get-tuple-element.16.gz_hbm, ...), custom_call_target="tpu_custom_call" | custom-call | tf_op jit(solution)/shard_map/finish/pallas_call | solution.py:628

commit v5 on v4

--- a/solution.py
+++ b/solution.py
@@ -434,79 +434,79 @@
     pl.semaphore_wait(barrier, len(peers))
 
     send_far(0)
+    send_w(0)
+    send_x(0)
+    send_w(1)
     send_w(2)
-    send_w(0)
-    send_w(1)
-    relay_w(2)
-    pass_first(2)
-    send_x(0)
-    pass_x(0)
     pass_first(0)
     relay_w(0)
+    relay_w(1)
+    forward_first(0)
+    pass_first(1)
+    pass_x(0)
+    relay_w(2)
+    send_g(2)
+    pass_second(0)
+    pass_first(2)
+    send_g(1)
     send_x(1)
+    forward_second(0)
+    send_far(1)
+    forward_own(0)
+    pass_second(1)
+    forward_first(1)
+    forward_far(0)
     pass_second(2)
-    pass_first(1)
-    relay_w(1)
-    send_g(1)
+    forward_first(2)
     send_g(0)
-    forward_far(0)
-    forward_first(0)
-    pass_second(0)
-    forward_own(0)
+    send_g(ATTN)
+    forward_second(1)
+    pass_g(2)
     forward_second(2)
-    forward_first(1)
-    send_far(1)
-    pass_second(1)
-    forward_second(0)
+    term(2, 0)
     pass_g(1)
-    forward_second(1)
-    forward_first(2)
+    forward_own(1)
+    term(2, 1)
+    term(1, 1)
+    pass_x(1)
+    combine(2, 0)
     term(1, 0)
-    term(1, 1)
     pass_g(0)
-    forward_own(1)
-    send_g(2)
+    combine(2, 1)
+    combine(1, 1)
+    sum_y(2, 0)
     combine(1, 0)
-    pass_x(1)
+    forward_far(1)
     term(0, 0)
-    send_g(ATTN)
     term(0, 1)
-    pass_g(2)
-    combine(1, 1)
+    sum_y(1, 1)
+    sum_y(2, 1)
+    pass_g(ATTN)
+    input_term(0)
     combine(0, 0)
+    term(ATTN, 0)
     sum_y(1, 0)
-    forward_far(1)
     combine(0, 1)
-    term(2, 1)
-    pass_g(ATTN)
-    term(2, 0)
+    input_term(1)
+    relay_z(2, 1)
+    combine(ATTN, 0)
     sum_y(0, 0)
-    sum_y(1, 1)
+    term(ATTN, 1)
+    gi_combine(0)
+    relay_z(2, 0)
     sum_y(0, 1)
-    combine(2, 1)
-    term(ATTN, 0)
+    relay_z(1, 1)
     relay_z(1, 0)
-    input_term(0)
-    combine(2, 0)
-    sum_y(2, 1)
-    combine(ATTN, 0)
-    term(ATTN, 1)
-    relay_z(1, 1)
-    sum_y(2, 0)
-    relay_z(0, 0)
     sum_y(ATTN, 0)
-    relay_z(0, 1)
-    gi_combine(0)
     combine(ATTN, 1)
     sum_y(ATTN, 1)
-    relay_z(2, 0)
+    relay_z(0, 0)
+    gi_combine(1)
+    relay_z(0, 1)
     sum_x(0)
-    relay_z(2, 1)
-    input_term(1)
+    relay_z(ATTN, 1)
+    sum_x(1)
     relay_z(ATTN, 0)
-    relay_z(ATTN, 1)
-    gi_combine(1)
-    sum_x(1)
 
     gi_far().wait_recv()
     for a in (0, 1, 2, ATTN):

time: 107 us -> 106 us (level)
  no operation moved by 1% of the time
where the time goes in v5:
time: 106 us
  Pallas kernels  105 us (99%)
    pallas_call x1, Pallas kernels, local(): pl.pallas_call(exchange_kernel, name='exchange', out_shape=(jax.ShapeDtyp...  103 us
    pallas_call x1, Pallas kernels, local(): pl.pallas_call(finish_kernel, name='finish', out_shape=(jax.ShapeDtypeStr...  2.29 us

profile of v5, /device:TPU:1, one launch (start us, length us, event | category | flops | bytes accessed | tf_op | source)
XLA Modules:
  0.0 106.0 jit_solution(11316164447322318396)
XLA Ops:
  0.6 103.1 %exchange.1 = (bf16[3,2,512,128]{3,2,1,0:T(8,128)(2,1)}, bf16[2,128,512]{2,1,0:T(8,128)(2,1)}, bf16[256,512]{1,0:T(8,128)(2,1)}, f32[256,512]{1,0:T(8,128)}) custom-call(bf16[256,512]{1,0:T(8,128)(2,1)} %bitcast.7, bf16[256,512]{1,0:T(8,128)(2,1)} %bitcast.8, bf16[1024,128]{1,0:T(8,128)(2,1)} %bitcast.9, bf16[1024,128]{1,0:T(8,128)(2,1)} %bitcast.10, ...), custom_call_target="tpu_custom_call" | custom-call | tf_op jit(solution)/shard_map/exchange/pallas_call | solution.py:569
  103.8 2.3 %finish.1 = (bf16[256,512]{1,0:T(8,128)(2,1)}, f32[512,128]{1,0:T(8,128)}, f32[512,128]{1,0:T(8,128)}, f32[512,128]{1,0:T(8,128)}, f32[128,512]{1,0:T(8,128)}) custom-call(bf16[3,2,512,128]{3,2,1,0:T(8,128)(2,1)} %get-tuple-element.14.zr_hbm, bf16[2,128,512]{2,1,0:T(8,128)(2,1)} %get-tuple-element.15.zro_hbm, bf16[256,512]{1,0:T(8,128)(2,1)} %get-tuple-element.16.gz_hbm, ...), custom_call_target="tpu_custom_call" | custom-call | tf_op jit(solution)/shard_map/finish/pallas_call | solution.py:628
